TPU v7x, 32 devices: a whole 2x2x4 slice. The times are simulated.
32 devices in a mesh: dp: 16 (over z, x, core), tensor: 2 (over y).
Axes of the slice: x: 2, y: 2, z: 4, core: 2. Of those that a mesh axis runs over, the one named last changes fastest.
Arguments:
- latents: float32 [128, 256, 1152], P('dp'), may hold values from -8 to 8
- cotangent: float32 [128, 256, 1152], P('dp'), may hold values from -8 to 8
- timesteps: int32 [128], P('dp'), may hold values from 0 to 999
- labels: int32 [128], P('dp'), may hold values from 0 to 1000
- label_table: float32 [1001, 1152], replicated, may hold values from -6 to 6
- modulate_w: float32 [1152, 6, 1152], P('dp', None, 'tensor'), may hold values from -0.1875 to 0.1875
- attend_w: float32 [1152, 3, 1152], P('dp', None, 'tensor'), may hold values from -0.1875 to 0.1875
- output_projection_weight: float32 [1152, 1152], P('tensor', 'dp'), may hold values from -0.75 to 0.75
- expand_w: float32 [1152, 4, 1152], P('dp', None, 'tensor'), may hold values from -0.1875 to 0.1875
- contract_w: float32 [4, 1152, 1152], P(None, 'tensor', 'dp'), may hold values from -0.09375 to 0.09375
- units_bias: float32 [12, 1152], P(None, 'tensor'), may hold values from -1.75 to 1.75
- output_width_bias: float32 [2, 1152], replicated, may hold values from -1.75 to 1.75
- modulate_mean: float32 [1152, 6, 1152], P('dp', None, 'tensor'), may hold values from -128 to 128
- modulate_square: float32 [1152, 6, 1152], P('dp', None, 'tensor'), may hold values from 45.8752 to 190.0544
- attend_mean: float32 [1152, 3, 1152], P('dp', None, 'tensor'), may hold values from -160 to 160
- attend_square: float32 [1152, 3, 1152], P('dp', None, 'tensor'), may hold values from 65.536 to 262.144
- project_mean: float32 [1152, 1152], P('tensor', 'dp'), may hold values from -48 to 48
- project_square: float32 [1152, 1152], P('tensor', 'dp'), may hold values from 5.24288 to 20.97152
- expand_mean: float32 [1152, 4, 1152], P('dp', None, 'tensor'), may hold values from -80 to 80
- expand_square: float32 [1152, 4, 1152], P('dp', None, 'tensor'), may hold values from 16.384 to 65.536
- contract_mean: float32 [4, 1152, 1152], P(None, 'tensor', 'dp'), may hold values from -64 to 64
- contract_square: float32 [4, 1152, 1152], P(None, 'tensor', 'dp'), may hold values from 11.79648 to 47.18592
- units_mean: float32 [12, 1152], P(None, 'tensor'), may hold values from -128 to 128
- units_square: float32 [12, 1152], P(None, 'tensor'), may hold values from 32.768 to 131.072
- widths_mean: float32 [2, 1152], replicated, may hold values from -128 to 128
- widths_square: float32 [2, 1152], replicated, may hold values from 32.768 to 131.072
Outputs:
- block_out: float32 [128, 256, 1152], P('dp')
- latents_grad: float32 [128, 256, 1152], P('dp')
- cond_grad: float32 [128, 1152], P('dp')
- modulate_grad: float32 [1152, 6, 1152], P('dp', None, 'tensor')
- modulate_moment: float32 [1152, 6, 1152], P('dp', None, 'tensor')
- modulate_second: float32 [1152, 6, 1152], P('dp', None, 'tensor')
- modulate_next: float32 [1152, 6, 1152], P('dp', None, 'tensor')
- attend_grad: float32 [1152, 3, 1152], P('dp', None, 'tensor')
- attend_moment: float32 [1152, 3, 1152], P('dp', None, 'tensor')
- attend_second: float32 [1152, 3, 1152], P('dp', None, 'tensor')
- attend_next: float32 [1152, 3, 1152], P('dp', None, 'tensor')
- project_grad: float32 [1152, 1152], P('tensor', 'dp')
- project_moment: float32 [1152, 1152], P('tensor', 'dp')
- project_second: float32 [1152, 1152], P('tensor', 'dp')
- project_next: float32 [1152, 1152], P('tensor', 'dp')
- expand_grad: float32 [1152, 4, 1152], P('dp', None, 'tensor')
- expand_moment: float32 [1152, 4, 1152], P('dp', None, 'tensor')
- expand_second: float32 [1152, 4, 1152], P('dp', None, 'tensor')
- expand_next: float32 [1152, 4, 1152], P('dp', None, 'tensor')
- contract_grad: float32 [4, 1152, 1152], P(None, 'tensor', 'dp')
- contract_moment: float32 [4, 1152, 1152], P(None, 'tensor', 'dp')
- contract_second: float32 [4, 1152, 1152], P(None, 'tensor', 'dp')
- contract_next: float32 [4, 1152, 1152], P(None, 'tensor', 'dp')
- units_grad: float32 [12, 1152], P(None, 'tensor')
- units_moment: float32 [12, 1152], P(None, 'tensor')
- units_second: float32 [12, 1152], P(None, 'tensor')
- units_next: float32 [12, 1152], P(None, 'tensor')
- widths_grad: float32 [2, 1152], replicated
- widths_moment: float32 [2, 1152], replicated
- widths_second: float32 [2, 1152], replicated
- widths_next: float32 [2, 1152], replicated
All inputs are finite; a program needn't handle non-finite values.
Results may differ from a plain program's by a relative error of at most 0.017.
Values may be sent and summed in bfloat16 or wider, within the bound.
A program may use at most 320 MiB of HBM per device.

v0:
```python
import math

import jax
import jax.numpy as jnp
from jax import lax
from jax.sharding import PartitionSpec as P

D = 1152
HEAD_DIM = 72
FF = 4608
STEP = 10


BETA_ONE = 0.9
BETA_TWO = 0.999
ADAM_EPS = 1e-08
NORM_EPS = 1e-06
EXACT_PRECISION = lax.Precision.HIGHEST


def frequencies(stamps, features):
    half_count = features // 2
    freq_index = jnp.arange(half_count, dtype=jnp.float32)
    freq_rates = jnp.exp(freq_index * (-math.log(10000.0) / half_count))
    angles = stamps.astype(jnp.float32)[:, None] * freq_rates[None, :]
    return jnp.concatenate([jnp.cos(angles), jnp.sin(angles)], axis=1)


def normalize(rows_in):
    centred = rows_in - jnp.mean(rows_in, axis=-1, keepdims=True)
    inverse = lax.rsqrt(jnp.mean(jnp.square(centred), axis=-1, keepdims=True) + NORM_EPS)
    return (centred * inverse, inverse)


def norm_back(normed, inverse, upstream):
    return inverse * (
        upstream
        - jnp.mean(upstream, axis=-1, keepdims=True)
        - normed * jnp.mean(upstream * normed, axis=-1, keepdims=True)
    )


def gelu_tanh(rows_in):
    return jax.nn.gelu(rows_in, approximate=True)


def local_grad(mapping, rows_in, upstream):
    return jax.vjp(mapping, rows_in)[1](upstream)[0]


def adam(weight, first_old, second_old, upstream, step_rate):
    first_new = BETA_ONE * first_old + (1.0 - BETA_ONE) * upstream
    second_new = BETA_TWO * second_old + (1.0 - BETA_TWO) * upstream * upstream
    fixed_first = first_new / (1.0 - BETA_ONE**STEP)
    fixed_second = second_new / (1.0 - BETA_TWO**STEP)
    return (
        first_new,
        second_new,
        weight - step_rate * fixed_first / (jnp.sqrt(fixed_second) + ADAM_EPS),
    )


def on_device(
    latents,
    cotangent,
    timesteps,
    labels,
    label_table,
    modulate_w,
    attend_w,
    output_projection_weight,
    expand_w,
    contract_w,
    units_bias,
    output_width_bias,
    modulate_mean,
    modulate_square,
    attend_mean,
    attend_square,
    project_mean,
    project_square,
    expand_mean,
    expand_square,
    contract_mean,
    contract_square,
    units_mean,
    units_square,
    widths_mean,
    widths_square,
):
    latent_count, length, features = latents.shape
    half_width = attend_w.shape[2]
    blocks = expand_w.shape[1]
    heads_here = half_width // HEAD_DIM
    tokens = latent_count * length
    score_scale = HEAD_DIM ** (-0.5)
    head_shape = (latent_count, length, heads_here, HEAD_DIM)
    onehot = (labels[:, None] == jnp.arange(label_table.shape[0], dtype=jnp.int32)[None, :]).astype(
        jnp.float32
    )
    condition = jnp.dot(onehot, label_table, precision=EXACT_PRECISION) + frequencies(
        timesteps, features
    )
    cond_low = jax.nn.silu(condition).astype(jnp.bfloat16)
    mod_low = modulate_w.astype(jnp.bfloat16)
    attend_low = attend_w.astype(jnp.bfloat16)
    project_low = output_projection_weight.astype(jnp.bfloat16)
    expand_low = expand_w.astype(jnp.bfloat16)
    contract_low = contract_w.astype(jnp.bfloat16)
    mod_bias = units_bias[:6][None]
    full_mod, full_attend, full_project, full_expand, full_contract = (
        lax.all_gather(mod_low, "dp", axis=0, tiled=True),
        lax.all_gather(attend_low, "dp", axis=0, tiled=True),
        lax.all_gather(project_low, "dp", axis=1, tiled=True),
        lax.all_gather(expand_low, "dp", axis=0, tiled=True),
        lax.all_gather(contract_low, "dp", axis=2, tiled=True),
    )
    mod_half = (
        jnp.einsum("ld,dkf->lkf", cond_low, full_mod, preferred_element_type=jnp.float32) + mod_bias
    )
    modulation = lax.all_gather(mod_half, "tensor", axis=2, tiled=True)
    pieces = [modulation[:, part_index][:, None, :] for part_index in range(6)]
    shift_one, scale_one, gate_one, shift_two, scale_two, gate_two = pieces
    normed_one, inverse_one = normalize(latents)
    flat_one = (
        (normed_one * (1.0 + scale_one) + shift_one).astype(jnp.bfloat16).reshape(tokens, features)
    )
    projected = jnp.einsum("td,dkf->tkf", flat_one, full_attend, preferred_element_type=jnp.float32)
    query_heads = (projected[:, 0] + units_bias[6]).astype(jnp.bfloat16).reshape(head_shape)
    key_heads = projected[:, 1].astype(jnp.bfloat16).reshape(head_shape)
    value_heads = (projected[:, 2] + units_bias[7]).astype(jnp.bfloat16).reshape(head_shape)
    scores = (
        jnp.einsum("lqhe,lkhe->lhqk", query_heads, key_heads, preferred_element_type=jnp.float32)
        * score_scale
    )
    row_peak = jnp.max(scores, axis=-1, keepdims=True)
    raised = jnp.exp(scores - row_peak)
    row_total = jnp.sum(raised, axis=-1, keepdims=True)
    log_total = row_peak + jnp.log(row_total)
    probs_low = (raised / row_total).astype(jnp.bfloat16)
    merged_head_values = jnp.einsum(
        "lhqk,lkhe->lqhe", probs_low, value_heads, preferred_element_type=jnp.float32
    )
    mixed_low = merged_head_values.reshape(tokens, half_width).astype(jnp.bfloat16)
    attn_part = jnp.dot(mixed_low, full_project, preferred_element_type=jnp.float32)
    attention_output = (
        lax.psum(attn_part.astype(jnp.bfloat16), "tensor").astype(jnp.float32)
        + output_width_bias[0]
    ).reshape(latent_count, length, features)
    after_attn = latents + gate_one * attention_output
    normed_two, inverse_two = normalize(after_attn)
    input_two = (
        (normed_two * (1.0 + scale_two) + shift_two).astype(jnp.bfloat16).reshape(tokens, features)
    )
    expand_flat = full_expand.reshape(features, blocks * half_width)
    contract_flat = full_contract.reshape(blocks * half_width, features)
    hidden_pre = jnp.dot(input_two, expand_flat, preferred_element_type=jnp.float32) + units_bias[
        8:
    ].reshape(blocks * half_width)
    hidden_low = gelu_tanh(hidden_pre).astype(jnp.bfloat16)
    mlp_part = jnp.dot(hidden_low, contract_flat, preferred_element_type=jnp.float32)
    contracted = (
        lax.psum(mlp_part.astype(jnp.bfloat16), "tensor").astype(jnp.float32) + output_width_bias[1]
    ).reshape(latent_count, length, features)
    block_out = after_attn + gate_two * contracted
    gate_two_grad = jnp.sum(cotangent * contracted, axis=1)
    contract_in = (gate_two * cotangent).astype(jnp.bfloat16).reshape(tokens, features)
    width_bias_two = jnp.sum(contract_in, axis=0, dtype=jnp.float32)
    contract_local = jnp.einsum(
        "th,te->he", hidden_low, contract_in, preferred_element_type=jnp.float32
    ).reshape(blocks, half_width, features)
    hidden_grad = jnp.einsum(
        "te,he->th", contract_in, contract_flat, preferred_element_type=jnp.float32
    )
    expand_in = local_grad(gelu_tanh, hidden_pre, hidden_grad).astype(jnp.bfloat16)
    unit_bias_hidden = jnp.sum(expand_in, axis=0, dtype=jnp.float32).reshape(blocks, half_width)
    expand_local = jnp.einsum(
        "td,th->dh", input_two, expand_in, preferred_element_type=jnp.float32
    ).reshape(features, blocks, half_width)
    input_two_part = jnp.einsum(
        "th,dh->td", expand_in, expand_flat, preferred_element_type=jnp.float32
    )
    input_two_grad = (
        lax.psum(input_two_part.astype(jnp.bfloat16), "tensor")
        .astype(jnp.float32)
        .reshape(latent_count, length, features)
    )
    scale_two_grad = jnp.sum(input_two_grad * normed_two, axis=1)
    shift_two_grad = jnp.sum(input_two_grad, axis=1)
    after_grad = cotangent + norm_back(normed_two, inverse_two, input_two_grad * (1.0 + scale_two))
    gate_one_grad = jnp.sum(after_grad * attention_output, axis=1)
    attn_in = (gate_one * after_grad).astype(jnp.bfloat16).reshape(tokens, features)
    width_bias_one = jnp.sum(attn_in, axis=0, dtype=jnp.float32)
    project_local = jnp.einsum("tf,te->fe", mixed_low, attn_in, preferred_element_type=jnp.float32)
    mixed_grad = (
        jnp.einsum("te,fe->tf", attn_in, full_project, preferred_element_type=jnp.float32)
        .astype(jnp.bfloat16)
        .reshape(head_shape)
    )
    scores_again = (
        jnp.einsum("lqhe,lkhe->lhqk", query_heads, key_heads, preferred_element_type=jnp.float32)
        * score_scale
    )
    attn_probs = jnp.exp(scores_again - log_total)
    probs_again = attn_probs.astype(jnp.bfloat16)
    value_grad = jnp.einsum(
        "lhqk,lqhe->lkhe", probs_again, mixed_grad, preferred_element_type=jnp.float32
    ).astype(jnp.bfloat16)
    probs_grad = jnp.einsum(
        "lqhe,lkhe->lhqk", mixed_grad, value_heads, preferred_element_type=jnp.float32
    )
    scores_grad = (
        attn_probs * (probs_grad - jnp.sum(attn_probs * probs_grad, axis=-1, keepdims=True))
    ).astype(jnp.bfloat16)
    query_grad = (
        jnp.einsum("lhqk,lkhe->lqhe", scores_grad, key_heads, preferred_element_type=jnp.float32)
        * score_scale
    ).astype(jnp.bfloat16)
    key_grad = (
        jnp.einsum("lhqk,lqhe->lkhe", scores_grad, query_heads, preferred_element_type=jnp.float32)
        * score_scale
    ).astype(jnp.bfloat16)
    query_flat = query_grad.reshape(tokens, half_width)
    value_flat = value_grad.reshape(tokens, half_width)
    qkv_grad = jnp.stack([query_flat, key_grad.reshape(tokens, half_width), value_flat], axis=1)
    unit_bias_query = jnp.sum(query_flat, axis=0, dtype=jnp.float32)
    unit_bias_value = jnp.sum(value_flat, axis=0, dtype=jnp.float32)
    attend_local = jnp.einsum("td,tkf->dkf", flat_one, qkv_grad, preferred_element_type=jnp.float32)
    input_one_part = jnp.einsum(
        "tkf,dkf->td", qkv_grad, full_attend, preferred_element_type=jnp.float32
    )
    input_one_grad = (
        lax.psum(input_one_part.astype(jnp.bfloat16), "tensor")
        .astype(jnp.float32)
        .reshape(latent_count, length, features)
    )
    scale_one_grad = jnp.sum(input_one_grad * normed_one, axis=1)
    shift_one_grad = jnp.sum(input_one_grad, axis=1)
    latents_grad = after_grad + norm_back(
        normed_one, inverse_one, input_one_grad * (1.0 + scale_one)
    )
    mod_grad = jnp.stack(
        [
            shift_one_grad,
            scale_one_grad,
            gate_one_grad,
            shift_two_grad,
            scale_two_grad,
            gate_two_grad,
        ],
        axis=1,
    ).astype(jnp.bfloat16)
    mod_grad_half = lax.dynamic_slice_in_dim(
        mod_grad, lax.axis_index("tensor") * half_width, half_width, 2
    )
    unit_bias_mod = jnp.sum(mod_grad_half, axis=0, dtype=jnp.float32)
    mod_local = jnp.einsum(
        "ld,lkf->dkf", cond_low, mod_grad_half, preferred_element_type=jnp.float32
    )
    cond_part = jnp.einsum(
        "lkf,dkf->ld", mod_grad_half, full_mod, preferred_element_type=jnp.float32
    )
    modulate_grad, attend_grad, project_grad, expand_grad, contract_grad = (
        lax.psum_scatter(mod_local, "dp", scatter_dimension=0, tiled=True),
        lax.psum_scatter(attend_local, "dp", scatter_dimension=0, tiled=True),
        lax.psum_scatter(project_local, "dp", scatter_dimension=1, tiled=True),
        lax.psum_scatter(expand_local, "dp", scatter_dimension=0, tiled=True),
        lax.psum_scatter(contract_local, "dp", scatter_dimension=2, tiled=True),
    )
    cond_sum = lax.psum(cond_part.astype(jnp.bfloat16), "tensor").astype(jnp.float32)
    cond_grad = local_grad(jax.nn.silu, condition, cond_sum)
    units_local = jnp.concatenate(
        [unit_bias_mod, unit_bias_query[None], unit_bias_value[None], unit_bias_hidden], axis=0
    )
    widths_local = jnp.stack([width_bias_one, width_bias_two], axis=0)
    units_grad, widths_grad = lax.psum((units_local, widths_local), "dp")
    m_mod, s_mod, n_mod = adam(
        modulate_w, modulate_mean, modulate_square, modulate_grad, D ** (-0.5)
    )
    m_att, s_att, n_att = adam(attend_w, attend_mean, attend_square, attend_grad, D ** (-0.5))
    m_proj, s_proj, n_proj = adam(
        output_projection_weight, project_mean, project_square, project_grad, (D // 16) ** (-0.5)
    )
    m_exp, s_exp, n_exp = adam(expand_w, expand_mean, expand_square, expand_grad, D ** (-0.5))
    m_con, s_con, n_con = adam(
        contract_w, contract_mean, contract_square, contract_grad, FF ** (-0.5)
    )
    m_units, s_units, n_units = adam(units_bias, units_mean, units_square, units_grad, 0.15)
    m_widths, s_widths, n_widths = adam(
        output_width_bias, widths_mean, widths_square, widths_grad, 0.15
    )
    return (
        block_out,
        latents_grad,
        cond_grad,
        modulate_grad,
        m_mod,
        s_mod,
        n_mod,
        attend_grad,
        m_att,
        s_att,
        n_att,
        project_grad,
        m_proj,
        s_proj,
        n_proj,
        expand_grad,
        m_exp,
        s_exp,
        n_exp,
        contract_grad,
        m_con,
        s_con,
        n_con,
        units_grad,
        m_units,
        s_units,
        n_units,
        widths_grad,
        m_widths,
        s_widths,
        n_widths,
    )


def solution(mesh):
    placed = (
        P("dp", None, None),
        P("dp", None, None),
        P("dp"),
        P("dp"),
        P(),
        P("dp", None, "tensor"),
        P("dp", None, "tensor"),
        P("tensor", "dp"),
        P("dp", None, "tensor"),
        P(None, "tensor", "dp"),
        P(None, "tensor"),
        P(),
        P("dp", None, "tensor"),
        P("dp", None, "tensor"),
        P("dp", None, "tensor"),
        P("dp", None, "tensor"),
        P("tensor", "dp"),
        P("tensor", "dp"),
        P("dp", None, "tensor"),
        P("dp", None, "tensor"),
        P(None, "tensor", "dp"),
        P(None, "tensor", "dp"),
        P(None, "tensor"),
        P(None, "tensor"),
        P(),
        P(),
    )
    return jax.shard_map(
        on_device,
        mesh=mesh,
        in_specs=placed,
        out_specs=(
            P("dp", None, None),
            P("dp", None, None),
            P("dp", None),
            P("dp", None, "tensor"),
            P("dp", None, "tensor"),
            P("dp", None, "tensor"),
            P("dp", None, "tensor"),
            P("dp", None, "tensor"),
            P("dp", None, "tensor"),
            P("dp", None, "tensor"),
            P("dp", None, "tensor"),
            P("tensor", "dp"),
            P("tensor", "dp"),
            P("tensor", "dp"),
            P("tensor", "dp"),
            P("dp", None, "tensor"),
            P("dp", None, "tensor"),
            P("dp", None, "tensor"),
            P("dp", None, "tensor"),
            P(None, "tensor", "dp"),
            P(None, "tensor", "dp"),
            P(None, "tensor", "dp"),
            P(None, "tensor", "dp"),
            P(None, "tensor"),
            P(None, "tensor"),
            P(None, "tensor"),
            P(None, "tensor"),
            P(),
            P(),
            P(),
            P(),
        ),
        check_vma=False,
    )
```

profile of v0, /device:TPU:0, one launch (start us, length us, event | category | flops | bytes accessed | tf_op | source)
XLA Modules:
  0.0 1636.0 jit_solution(8726826336073443521)
XLA Ops:
  32.3 59.0 %all-gather.6.cloned.1.call-done = bf16[1152,6,576]{2,0,1:T(8,128)(2,1)} async-done(((bf16[72,6,576]{2,0,1:T(8,128)(2,1)}), bf16[1152,6,576]{2,0,1:T(8,128)(2,1)}) %all-gather.6.cloned.1.call-update) | async-done | bytes 7962640 | tf_op jit(solution)/shard_map/all_gather | solution.py:112
  97.0 54.4 %all_gather.19 = f32[8,6,1152]{1,0,2:T(8,128)} all-gather(f32[8,6,576]{1,0,2:T(8,128)S(1)} %copy.143), channel_id=1, replica_groups=mesh['dp'=16,'tensor'=2] {'tensor'}, dimensions={2}, use_global_device_ids=true | all-gather | bytes 331776 | tf_op jit(solution)/shard_map/all_gather | solution.py:121
  151.4 22.2 %fusion.85 = (f32[8,1,1152]{1,0,2:T(8,128)}, f32[8,1,1152]{1,0,2:T(8,128)}, f32[8,1,1152]{1,0,2:T(8,128)}, f32[8,1,1152]{1,0,2:T(8,128)}, f32[8,1,1152]{1,0,2:T(8,128)}, /*index=5*/f32[8,1,1152]{1,0,2:T(8,128)}) fusion(f32[8,6,1152]{1,0,2:T(8,128)} %all_gather.19), kind=kLoop, calls=%fused_computation.183 | loop fusion | bytes 442368 | tf_op jit(solution)/shard_map/slice | solution.py:122
  187.3 13.2 fusion.86
  266.5 40.6 %all-gather.14.cloned.1.call-done = bf16[4,576,1152]{1,0,2:T(4,128)(2,1)} async-done(((bf16[4,576,72]{1,0,2:T(4,128)(2,1)}), bf16[4,576,1152]{1,0,2:T(4,128)(2,1)}) %all-gather.14.cloned.1.call-update) | async-done | bytes 5308432 | tf_op jit(solution)/shard_map/all_gather | solution.py:116
  340.5 86.7 %all-reduce.7.cloned.1.call-done = bf16[2048,1152]{1,0:T(8,128)(2,1)} async-done(((bf16[2048,1152]{1,0:T(8,128)(2,1)}), bf16[2048,1152]{1,0:T(8,128)(2,1)}) %all-reduce.7.cloned.1.call-update) | async-done | bytes 4718608 | tf_op jit(solution)/shard_map/psum | solution.py:147
  453.5 16.1 fusion.87
  469.6 34.6 %convert_reduce_fusion = (f32[2304]{0:T(1024)}, bf16[2048,2304]{1,0:T(8,128)(2,1)}, f32[2048,2304]{1,0:T(8,128)}) fusion(f32[2048,2304]{1,0:T(8,128)} %fusion.87, f32[2304]{0:T(1024)S(1)} %add.290, bf16[2048,1152]{1,0:T(8,128)(2,1)} %bitcast.214, bf16[2304,1152]{1,0:T(8,128)(2,1)S(1)} %bitcast.207), kind=kOutput, calls=%fused_computation.25 | convolution fusion | flops 10980161536 | bytes 57231360 | tf_op jit(solution)/shard_map/te,he->th/dot_general | solution.py:172
  504.3 15.8 convolution_convert_fusion.1
  520.2 23.7 %fusion.30 = bf16[2048,1152]{1,0:T(8,128)(2,1)} fusion(bf16[2304,1152]{1,0:T(8,128)(2,1)} %bitcast.204, f32[2048,2304]{1,0:T(8,128)} %fusion.87, f32[2304]{0:T(1024)S(1)} %add.290), kind=kOutput, calls=%fused_computation.71 | convolution fusion | flops 10921181184 | bytes 28910592 | tf_op jit(solution)/shard_map/dot_general | solution.py:161
  543.9 95.6 %all-reduce.9.cloned.1.call-done = bf16[2048,1152]{1,0:T(8,128)(2,1)} async-done(((bf16[2048,1152]{1,0:T(8,128)(2,1)}), bf16[2048,1152]{1,0:T(8,128)(2,1)}) %all-reduce.9.cloned.1.call-update) | async-done | bytes 4718608 | tf_op jit(solution)/shard_map/psum | solution.py:184
  683.4 14.9 multiply_reduce_fusion
  753.5 13.2 bitcast_convert_fusion
  776.2 26.0 %fusion.14 = (bf16[2304,2048]{0,1:T(8,128)(2,1)}, bf16[2304,2048]{0,1:T(8,128)(2,1)}) fusion(f32[2048,2304]{1,0:T(8,128)} %fusion.87, f32[2304]{0:T(1024)S(1)} %add.290, f32[2048,2304]{1,0:T(8,128)} %get-tuple-element.215), kind=kLoop, calls=%fused_computation.20 | loop fusion | flops 108527616 | bytes 56632320 | tf_op jit(solution)/shard_map/convert_element_type | solution.py:160
  815.0 20.3 %fusion.90 = f32[1152,4,576]{2,0,1:T(8,128)} fusion(bf16[2048,1152,1]{1,0,2:T(8,128)(2,1)} %bitcast.219, bf16[4,576,2048]{2,1,0:T(8,128)(2,1)} %bitcast.200), kind=kOutput, calls=%fused_computation.188 | convolution fusion | flops 10871635968 | bytes 24772608 | tf_op jit(solution)/shard_map/td,th->dh/dot_general | solution.py:177
  848.2 20.2 %fusion.91 = f32[4,576,1152]{1,2,0:T(8,128)} fusion(bf16[4,576,2048]{2,1,0:T(8,128)(2,1)} %bitcast.201, bf16[2048,1152,1]{1,0,2:T(8,128)(2,1)} %bitcast.215), kind=kOutput, calls=%fused_computation.189 | convolution fusion | flops 10871635968 | bytes 24772608 | tf_op jit(solution)/shard_map/th,te->he/dot_general | solution.py:169
  868.5 16.6 %fusion.88 = f32[1152,3,576]{2,0,1:T(8,128)} fusion(bf16[2048,1152,1]{1,0,2:T(8,128)(2,1)} %bitcast.217, bf16[2048,3,576]{0,2,1:T(8,128)(2,1)} %copy-done.20), kind=kOutput, calls=%fused_computation.186 | convolution fusion | flops 8153726976 | bytes 19759104 | tf_op jit(solution)/shard_map/td,tkf->dkf/dot_general | solution.py:228
  885.1 102.8 %all-reduce.11.cloned.1.call-done = (bf16[2048,1152]{1,0:T(8,128)(2,1)}, bf16[2048,1152]{1,0:T(8,128)(2,1)}) async-done(((bf16[2048,1152]{1,0:T(8,128)(2,1)}, bf16[2048,1152]{1,0:T(8,128)(2,1)}), (bf16[2048,1152]{1,0:T(8,128)(2,1)}, bf16[2048,1152]{1,0:T(8,128)(2,1)})) %all-reduce.11.cloned.1.call-update) | async-done | bytes 9437200 | tf_op jit(solution)/shard_map/psum | solution.py:163
  1034.0 23.8 %reduce-scatter.16.cloned.1.call-done = f32[576,72]{0,1:T(8,128)} async-done(((f32[576,1152]{0,1:T(8,128)}), f32[576,72]{0,1:T(8,128)}) %reduce-scatter.16.cloned.1.call-update) | async-done | bytes 165904
  1059.7 60.1 %all-reduce.1 = (f32[12,576]{1,0:T(8,128)S(1)}, f32[2,1152]{1,0:T(2,128)S(1)}) all-reduce(f32[12,576]{1,0:T(8,128)S(1)} %pad_maximum_fusion, f32[2,1152]{1,0:T(2,128)S(1)} %pad_maximum_fusion.1), channel_id=1, replica_groups=mesh['dp'=16,'tensor'=2] {'dp'}, use_global_device_ids=true, to_apply=%region_31.32 | all-reduce | flops 9216 | bytes 73728 | tf_op jit(solution)/shard_map/psum | solution.py:276
  1147.5 42.1 %reduce-scatter.12.cloned.1.call-done = f32[72,4,576]{2,0,1:T(8,128)} async-done(((f32[1152,4,576]{2,0,1:T(8,128)}), f32[72,4,576]{2,0,1:T(8,128)}) %reduce-scatter.12.cloned.1.call-update) | async-done | bytes 663568 | tf_op jit(solution)/shard_map/reduce_scatter | solution.py:267
  1196.0 126.8 %reduce-scatter.14.cloned.1.call-done = f32[4,576,72]{1,2,0:T(8,128)} async-done(((f32[4,576,1152]{1,2,0:T(8,128)}), f32[4,576,72]{1,2,0:T(8,128)}) %reduce-scatter.14.cloned.1.call-update) | async-done | bytes 663568 | tf_op jit(solution)/shard_map/reduce_scatter | solution.py:268
  1326.0 108.2 %reduce-scatter.10.cloned.1.call-done = f32[72,3,576]{2,0,1:T(8,128)} async-done(((f32[1152,3,576]{2,0,1:T(8,128)}), f32[72,3,576]{2,0,1:T(8,128)}) %reduce-scatter.10.cloned.1.call-update) | async-done | bytes 497680 | tf_op jit(solution)/shard_map/reduce_scatter | solution.py:265
  1436.8 188.2 %reduce-scatter.8.cloned.1.call-done = f32[72,6,576]{2,0,1:T(8,128)} async-done(((f32[1152,6,576]{2,0,1:T(8,128)}), f32[72,6,576]{2,0,1:T(8,128)}) %reduce-scatter.8.cloned.1.call-update) | async-done | bytes 995344 | tf_op jit(solution)/shard_map/reduce_scatter | solution.py:264
  (300 shorter events, 395.4 us)
Async XLA Ops:
  7.2 84.1 %all-gather.6.cloned.1.call-start = ((), (), s32[]{:S(2)}) async-start(), calls=%async_computation.5 | async-start | bytes 9400320 | tf_op jit(solution)/shard_map/all_gather | solution.py:112
  9.4 177.9 %all-gather.8.cloned.1.call-start = ((), (), s32[]{:S(2)}) async-start(), calls=%async_computation.6 | async-start | bytes 4700160 | tf_op jit(solution)/shard_map/all_gather | solution.py:113
  11.2 234.5 %all-gather.10.cloned.1.call-start = ((), (), s32[]{:S(2)}) async-start(), calls=%async_computation.7 | async-start | bytes 1566720 | tf_op jit(solution)/shard_map/all_gather | solution.py:114
  12.9 241.7 %all-gather.12.cloned.1.call-start = ((), (), s32[]{:S(2)}) async-start(), calls=%async_computation.9 | async-start | bytes 6266880 | tf_op jit(solution)/shard_map/all_gather | solution.py:115
  15.0 292.1 %all-gather.14.cloned.1.call-start = ((), (), s32[]{:S(2)}) async-start(), calls=%async_computation.10 | async-start | bytes 6266880 | tf_op jit(solution)/shard_map/all_gather | solution.py:116
  17.1 410.1 %all-reduce.7.cloned.1.call-start = ((), (), s32[]{:S(2)}) async-start(), calls=%async_computation.8 | async-start | bytes 9437184 | tf_op jit(solution)/shard_map/psum | solution.py:147
  23.2 157.1 %copy-start.27 = (f32[8,256]{1,0:T(8,128)}, f32[8,256]{1,0:T(8,128)S(1)}, u32[]{:S(2)}) copy-start(f32[8,256]{1,0:T(8,128)S(1)} %broadcast_multiply_fusion.5) | copy-start | bytes 24580
  28.0 152.3 %copy-start.32 = (f32[8,256]{1,0:T(8,128)}, f32[8,256]{1,0:T(8,128)S(1)}, u32[]{:S(2)}) copy-start(f32[8,256]{1,0:T(8,128)S(1)} %add_rsqrt_fusion.1) | copy-start | bytes 24580
  28.1 207.2 %copy-start.44 = (f32[8,72]{1,0:T(8,128)}, f32[8,72]{1,0:T(8,128)S(1)}, u32[]{:S(2)}) copy-start(f32[8,72]{1,0:T(8,128)S(1)} %add.275) | copy-start | bytes 6916
  28.2 189.1 %copy-start.39 = (f32[8,72]{1,0:T(8,128)}, f32[8,72]{1,0:T(8,128)S(1)}, u32[]{:S(2)}) copy-start(f32[8,72]{1,0:T(8,128)S(1)} %add.278) | copy-start | bytes 6916
  253.8 385.6 %all-reduce.9.cloned.1.call-start = ((), (), s32[]{:S(2)}) async-start(), calls=%async_computation.11 | async-start | bytes 9437184 | tf_op jit(solution)/shard_map/psum | solution.py:184
  254.6 172.6 %copy-start.37 = (f32[1152]{0:T(1024)}, f32[1152]{0:T(1024)S(1)}, u32[]{:S(2)}) copy-start(f32[1152]{0:T(1024)S(1)} %get-tuple-element.164) | copy-start | bytes 13828
  520.1 467.9 %all-reduce.11.cloned.1.call-start = ((), (), s32[]{:S(2)}) async-start(), calls=%async_computation.17 | async-start | bytes 18874368 | tf_op jit(solution)/shard_map/psum | solution.py:163
  766.7 291.0 %reduce-scatter.16.cloned.1.call-start = ((), (), s32[]{:S(2)}) async-start(), calls=%async_computation.16 | async-start | bytes 3133440
  776.2 413.5 %reduce-scatter.12.cloned.1.call-start = ((), (), s32[]{:S(2)}) async-start(), calls=%async_computation.14 | async-start | bytes 12533760 | tf_op jit(solution)/shard_map/reduce_scatter | solution.py:267
  835.3 487.5 %reduce-scatter.14.cloned.1.call-start = ((), (), s32[]{:S(2)}) async-start(), calls=%async_computation.15 | async-start | bytes 12533760 | tf_op jit(solution)/shard_map/reduce_scatter | solution.py:268
  868.4 119.6 %copy-start.34 = (f32[1152]{0:T(1024)S(1)}, f32[1152]{0:T(1024)}, u32[]{:S(2)}) copy-start(f32[1152]{0:T(1024)} %get-tuple-element.163) | copy-start | bytes 13828
  868.4 565.8 %reduce-scatter.10.cloned.1.call-start = ((), (), s32[]{:S(2)}) async-start(), calls=%async_computation.13 | async-start | bytes 9400320 | tf_op jit(solution)/shard_map/reduce_scatter | solution.py:265
  885.1 109.5 %copy-start.19 = (f32[8,1152]{1,0:T(8,128)S(1)}, f32[8,1152]{1,0:T(8,128)}, u32[]{:S(2)}) copy-start(f32[8,1152]{1,0:T(8,128)} %copy-done.18) | copy-start | bytes 110596
  885.1 739.9 %reduce-scatter.8.cloned.1.call-start = ((), (), s32[]{:S(2)}) async-start(), calls=%async_computation.12 | async-start | bytes 18800640 | tf_op jit(solution)/shard_map/reduce_scatter | solution.py:264
  1147.4 175.3 %copy-start.13 = (f32[4,576,72]{1,2,0:T(8,128)S(1)}, f32[4,576,72]{1,2,0:T(8,128)}, u32[]{:S(2)}) copy-start(f32[4,576,72]{1,2,0:T(8,128)} %param.35) | copy-start | bytes 1990660
  1147.5 286.7 %copy-start.17 = (f32[72,3,576]{2,0,1:T(8,128)S(1)}, f32[72,3,576]{2,0,1:T(8,128)}, u32[]{:S(2)}) copy-start(f32[72,3,576]{2,0,1:T(8,128)} %param.32) | copy-start | bytes 1492996
  1147.5 477.5 %copy-start.11 = (f32[72,6,576]{2,0,1:T(8,128)S(1)}, f32[72,6,576]{2,0,1:T(8,128)}, u32[]{:S(2)}) copy-start(f32[72,6,576]{2,0,1:T(8,128)} %param.31) | copy-start | bytes 2985988
  1191.8 242.4 %copy-start.24 = (f32[72,3,576]{2,0,1:T(8,128)S(1)}, f32[72,3,576]{2,0,1:T(8,128)}, u32[]{:S(2)}) copy-start(f32[72,3,576]{2,0,1:T(8,128)} %param.41) | copy-start | bytes 1492996
  (65 other events, 1450.3 us)
Sparse Core Ops, SparseCore 0:
  10.8 80.4 all-gather.5
  94.1 49.9 all-gather.7
  146.8 37.8 all-gather.9
  187.4 58.5 all-gather.11
  248.7 58.3 all-gather.13
  309.4 117.8 all-reduce.6
  520.2 119.2 all-reduce.8
  766.8 221.1 all-reduce.10
  992.5 65.2 reduce-scatter.15
  1061.7 127.8 reduce-scatter.11
  1194.9 127.8 reduce-scatter.13
  1327.4 106.7 reduce-scatter.9
  1439.5 185.4 reduce-scatter.7
where the time goes:
time: 1640 us
  waiting for transfers between devices  874 us (53%)
  matrix products  271 us (17%)
  other arithmetic  193 us (12%)
  local copies, waits for them, and re-layouts  160 us (10%)
  blocking collectives  123 us (8%)
    reduce_scatter x1, waiting for transfers between devices, on_device(): lax.psum_scatter(mod_local, 'dp', scatter_dimension=0, tiled=True)  188 us
    reduce_scatter x1, waiting for transfers between devices, on_device(): lax.psum_scatter(contract_local, 'dp', scatter_dimension=2, tiled=True)  127 us
    reduce_scatter x1, waiting for transfers between devices, on_device(): lax.psum_scatter(attend_local, 'dp', scatter_dimension=0, tiled=True)  108 us
    psum x1, waiting for transfers between devices, on_device(): lax.psum(mlp_part.astype(jnp.bfloat16), 'tensor').astype(jnp.float32)  103 us
    psum x1, waiting for transfers between devices, on_device(): lax.psum(input_two_part.astype(jnp.bfloat16), 'tensor').astype(jnp.float32)  95.6 us
    psum x1, waiting for transfers between devices, on_device(): lax.psum(attn_part.astype(jnp.bfloat16), 'tensor').astype(jnp.float32)  86.7 us
    psum x1, blocking collectives, on_device(): units_grad, widths_grad = lax.psum((units_local, widths_local), 'dp')  60.1 us
    all_gather x1, waiting for transfers between devices, on_device(): lax.all_gather(mod_low, 'dp', axis=0, tiled=True)  59 us
  transfers between devices with their start and end apart: 13, of which 10 were waited for; matrix products, arithmetic and copies ran while one was open for 24% of the time, Pallas kernels for 0%

commit v1 on v0

v1 whole, which is shorter than its diff:
```python
import math

import jax
import jax.numpy as jnp
from jax import lax
from jax.experimental import pallas as pl
from jax.experimental.pallas import tpu as pltpu
from jax.sharding import PartitionSpec as P

D = 1152
HEAD_DIM = 72
FF = 4608
STEP = 10


BETA_ONE = 0.9
BETA_TWO = 0.999
ADAM_EPS = 1e-08
NORM_EPS = 1e-06
EXACT_PRECISION = lax.Precision.HIGHEST


def frequencies(stamps, features):
    half_count = features // 2
    freq_index = jnp.arange(half_count, dtype=jnp.float32)
    freq_rates = jnp.exp(freq_index * (-math.log(10000.0) / half_count))
    angles = stamps.astype(jnp.float32)[:, None] * freq_rates[None, :]
    return jnp.concatenate([jnp.cos(angles), jnp.sin(angles)], axis=1)


def normalize(rows_in):
    centred = rows_in - jnp.mean(rows_in, axis=-1, keepdims=True)
    inverse = lax.rsqrt(jnp.mean(jnp.square(centred), axis=-1, keepdims=True) + NORM_EPS)
    return (centred * inverse, inverse)


def norm_back(normed, inverse, upstream):
    return inverse * (
        upstream
        - jnp.mean(upstream, axis=-1, keepdims=True)
        - normed * jnp.mean(upstream * normed, axis=-1, keepdims=True)
    )


def gelu_tanh(rows_in):
    return jax.nn.gelu(rows_in, approximate=True)


def local_grad(mapping, rows_in, upstream):
    return jax.vjp(mapping, rows_in)[1](upstream)[0]


def adam(weight, first_old, second_old, upstream, step_rate):
    first_new = BETA_ONE * first_old + (1.0 - BETA_ONE) * upstream
    second_new = BETA_TWO * second_old + (1.0 - BETA_TWO) * upstream * upstream
    fixed_first = first_new / (1.0 - BETA_ONE**STEP)
    fixed_second = second_new / (1.0 - BETA_TWO**STEP)
    return (
        first_new,
        second_new,
        weight - step_rate * fixed_first / (jnp.sqrt(fixed_second) + ADAM_EPS),
    )


GROUPS = 2
VMEM_ASK = 48 * 1024 * 1024


def swap(piece):
    return lax.ppermute(piece, "tensor", [(0, 1), (1, 0)])


def pair_sum(part):
    return part.astype(jnp.float32) + swap(part).astype(jnp.float32)


def rows_dot(left, right):
    return lax.dot_general(
        left, right, (((1,), (0,)), ((), ())), preferred_element_type=jnp.float32
    )


def lanes_dot(left, right):
    return lax.dot_general(
        left, right, (((1,), (1,)), ((), ())), preferred_element_type=jnp.float32
    )


def tall_dot(left, right):
    return lax.dot_general(
        left, right, (((0,), (0,)), ((), ())), preferred_element_type=jnp.float32
    )


def head_probs(query, key):
    scores = lanes_dot(query, key) * (HEAD_DIM ** (-0.5))
    raised = jnp.exp(scores - jnp.max(scores, axis=-1, keepdims=True))
    return raised * (1.0 / jnp.sum(raised, axis=-1, keepdims=True))


def attend_kernel(qkv_ref, mixed_ref):
    width = mixed_ref.shape[-1]
    outs = []
    for head in range(width // HEAD_DIM):
        at = head * HEAD_DIM
        query = qkv_ref[0, :, at : at + HEAD_DIM]
        key = qkv_ref[0, :, width + at : width + at + HEAD_DIM]
        value = qkv_ref[0, :, 2 * width + at : 2 * width + at + HEAD_DIM]
        probs = head_probs(query, key).astype(jnp.bfloat16)
        outs.append(rows_dot(probs, value))
    mixed_ref[0] = jnp.concatenate(outs, axis=1).astype(jnp.bfloat16)


def attend_back_kernel(qkv_ref, up_ref, grad_ref):
    width = up_ref.shape[-1]
    score_scale = HEAD_DIM ** (-0.5)
    queries, keys, values = [], [], []
    for head in range(width // HEAD_DIM):
        at = head * HEAD_DIM
        query = qkv_ref[0, :, at : at + HEAD_DIM]
        key = qkv_ref[0, :, width + at : width + at + HEAD_DIM]
        value = qkv_ref[0, :, 2 * width + at : 2 * width + at + HEAD_DIM]
        upstream = up_ref[0, :, at : at + HEAD_DIM]
        probs = head_probs(query, key)
        values.append(tall_dot(probs.astype(jnp.bfloat16), upstream))
        probs_grad = lanes_dot(upstream, value)
        scores_grad = (
            probs * (probs_grad - jnp.sum(probs * probs_grad, axis=-1, keepdims=True))
        ).astype(jnp.bfloat16)
        queries.append(rows_dot(scores_grad, key) * score_scale)
        keys.append(tall_dot(scores_grad, query) * score_scale)
    grad_ref[0] = jnp.concatenate(queries + keys + values, axis=1).astype(jnp.bfloat16)


def per_latent(kernel, out_width, flops, *arrays):
    count, length = arrays[0].shape[:2]
    moved = sum(array.size for array in arrays) + count * length * out_width
    return pl.pallas_call(
        kernel,
        grid=(count,),
        out_shape=jax.ShapeDtypeStruct((count, length, out_width), jnp.bfloat16),
        in_specs=[
            pl.BlockSpec((1, length, array.shape[2]), lambda at: (at, 0, 0)) for array in arrays
        ],
        out_specs=pl.BlockSpec((1, length, out_width), lambda at: (at, 0, 0)),
        compiler_params=pltpu.CompilerParams(vmem_limit_bytes=VMEM_ASK),
        cost_estimate=pl.CostEstimate(
            flops=flops, bytes_accessed=2 * moved, transcendentals=count * length * length * 8
        ),
    )(*arrays)


def on_device(
    latents,
    cotangent,
    timesteps,
    labels,
    label_table,
    modulate_w,
    attend_w,
    output_projection_weight,
    expand_w,
    contract_w,
    units_bias,
    output_width_bias,
    modulate_mean,
    modulate_square,
    attend_mean,
    attend_square,
    project_mean,
    project_square,
    expand_mean,
    expand_square,
    contract_mean,
    contract_square,
    units_mean,
    units_square,
    widths_mean,
    widths_square,
):
    latent_count, length, features = latents.shape
    half_width = attend_w.shape[2]
    blocks = expand_w.shape[1]
    own_rows = attend_w.shape[0]
    hidden_units = blocks * half_width
    groups = GROUPS if latent_count % GROUPS == 0 else 1
    group_latents = latent_count // groups
    tokens = group_latents * length
    half_here = lax.axis_index("tensor")
    row_start = lax.axis_index("dp") * own_rows

    attend_rows = attend_w.astype(jnp.bfloat16).reshape(own_rows, 3 * half_width)
    project_rows = output_projection_weight.astype(jnp.bfloat16).T
    expand_rows = expand_w.astype(jnp.bfloat16).reshape(own_rows, hidden_units)
    contract_rows = (
        contract_w.astype(jnp.bfloat16).transpose(2, 0, 1).reshape(own_rows, hidden_units)
    )
    mod_rows = modulate_w.astype(jnp.bfloat16).reshape(own_rows, 6 * half_width)

    all_labels = lax.all_gather(labels, "dp", axis=0, tiled=True)
    all_stamps = lax.all_gather(timesteps, "dp", axis=0, tiled=True)
    own_table = lax.dynamic_slice_in_dim(label_table, row_start, own_rows, 1)
    onehot = (
        all_labels[:, None] == jnp.arange(label_table.shape[0], dtype=jnp.int32)[None, :]
    ).astype(jnp.float32)
    half_count = features // 2
    own_index = row_start + jnp.arange(own_rows, dtype=jnp.int32)
    own_rates = jnp.exp(
        (own_index % half_count).astype(jnp.float32) * (-math.log(10000.0) / half_count)
    )
    angles = all_stamps.astype(jnp.float32)[:, None] * own_rates[None, :]
    waves = jnp.where((own_index < half_count)[None, :], jnp.cos(angles), jnp.sin(angles))
    condition = jnp.dot(onehot, own_table, precision=EXACT_PRECISION) + waves
    cond_low = jax.nn.silu(condition).astype(jnp.bfloat16)
    mod_sum = lax.psum_scatter(
        rows_dot(cond_low, mod_rows), "dp", scatter_dimension=0, tiled=True
    )
    mod_half = mod_sum.reshape(latent_count, 6, half_width) + units_bias[:6][None]
    mod_other = swap(mod_half)
    modulation = jnp.where(
        half_here == 0,
        jnp.concatenate([mod_half, mod_other], axis=2),
        jnp.concatenate([mod_other, mod_half], axis=2),
    )

    full_attend = lax.all_gather(attend_rows, "dp", axis=0, tiled=True)
    full_project = lax.all_gather(project_rows, "dp", axis=0, tiled=True)
    full_expand = lax.all_gather(expand_rows, "dp", axis=0, tiled=True)
    full_contract = lax.all_gather(contract_rows, "dp", axis=0, tiled=True)
    qkv_bias = jnp.concatenate([units_bias[6], jnp.zeros_like(units_bias[6]), units_bias[7]])
    hidden_bias = units_bias[8:].reshape(hidden_units)
    attention_flops = 4 * tokens * length * half_width

    spans = [slice(g * group_latents, (g + 1) * group_latents) for g in range(groups)]
    lat = [latents[s] for s in spans]
    cot = [cotangent[s] for s in spans]
    mods = [[modulation[s, k][:, None, :] for k in range(6)] for s in spans]
    each = range(groups)

    norm_one, flat_one, qkv, mixed, attn_part = [], [], [], [], []
    for g in each:
        normed, inverse = normalize(lat[g])
        norm_one.append((normed, inverse))
        flat_one.append(
            (normed * (1.0 + mods[g][1]) + mods[g][0])
            .astype(jnp.bfloat16)
            .reshape(tokens, features)
        )
        qkv.append(
            (rows_dot(flat_one[g], full_attend) + qkv_bias)
            .astype(jnp.bfloat16)
            .reshape(group_latents, length, 3 * half_width)
        )
        mixed.append(
            per_latent(attend_kernel, half_width, attention_flops, qkv[g]).reshape(
                tokens, half_width
            )
        )
        attn_part.append(lanes_dot(mixed[g], full_project).astype(jnp.bfloat16))
    attn_sum = [pair_sum(attn_part[g]) for g in each]

    group_shape = (group_latents, length, features)
    attention_output, after_attn, norm_two, input_two = [], [], [], []
    mlp_part, contract_in, hidden_low, expand_in, input_two_part = [], [], [], [], []
    for g in each:
        attention_output.append((attn_sum[g] + output_width_bias[0]).reshape(group_shape))
        after_attn.append(lat[g] + mods[g][2] * attention_output[g])
        normed, inverse = normalize(after_attn[g])
        norm_two.append((normed, inverse))
        input_two.append(
            (normed * (1.0 + mods[g][4]) + mods[g][3])
            .astype(jnp.bfloat16)
            .reshape(tokens, features)
        )
        hidden_pre = rows_dot(input_two[g], full_expand) + hidden_bias
        hidden_low.append(gelu_tanh(hidden_pre).astype(jnp.bfloat16))
        contract_in.append((mods[g][5] * cot[g]).astype(jnp.bfloat16).reshape(tokens, features))
        hidden_grad = rows_dot(contract_in[g], full_contract)
        expand_in.append(local_grad(gelu_tanh, hidden_pre, hidden_grad).astype(jnp.bfloat16))
        input_two_part.append(lanes_dot(expand_in[g], full_expand).astype(jnp.bfloat16))
        mlp_part.append(lanes_dot(hidden_low[g], full_contract).astype(jnp.bfloat16))
    input_two_sum = [pair_sum(input_two_part[g]) for g in each]
    mlp_sum = [pair_sum(mlp_part[g]) for g in each]

    def summed_grad(lefts, rights):
        total = tall_dot(lefts[0], rights[0])
        for g in range(1, groups):
            total = total + tall_dot(lefts[g], rights[g])
        return total.astype(jnp.bfloat16)

    def scattered(local):
        return lax.psum_scatter(local, "dp", scatter_dimension=0, tiled=True).astype(jnp.float32)

    contract_own = scattered(summed_grad(contract_in, hidden_low))
    expand_own = scattered(summed_grad(input_two, expand_in))

    after_grad, attn_in, qkv_grad, input_one_part = [], [], [], []
    scale_two_grad, shift_two_grad, gate_one_grad = [], [], []
    for g in each:
        normed, inverse = norm_two[g]
        upstream = input_two_sum[g].reshape(group_shape)
        scale_two_grad.append(jnp.sum(upstream * normed, axis=1))
        shift_two_grad.append(jnp.sum(upstream, axis=1))
        after_grad.append(cot[g] + norm_back(normed, inverse, upstream * (1.0 + mods[g][4])))
        gate_one_grad.append(jnp.sum(after_grad[g] * attention_output[g], axis=1))
        attn_in.append(
            (mods[g][2] * after_grad[g]).astype(jnp.bfloat16).reshape(tokens, features)
        )
        mixed_grad = (
            rows_dot(attn_in[g], full_project)
            .astype(jnp.bfloat16)
            .reshape(group_latents, length, half_width)
        )
        qkv_grad.append(
            per_latent(
                attend_back_kernel, 3 * half_width, 3 * attention_flops, qkv[g], mixed_grad
            ).reshape(tokens, 3 * half_width)
        )
        input_one_part.append(lanes_dot(qkv_grad[g], full_attend).astype(jnp.bfloat16))
    input_one_sum = [pair_sum(input_one_part[g]) for g in each]
    project_own = scattered(summed_grad(attn_in, mixed))
    attend_own = scattered(summed_grad(flat_one, qkv_grad))

    block_out, gate_two_grad, latents_grad, scale_one_grad, shift_one_grad = [], [], [], [], []
    for g in each:
        contracted = (mlp_sum[g] + output_width_bias[1]).reshape(group_shape)
        block_out.append(after_attn[g] + mods[g][5] * contracted)
        gate_two_grad.append(jnp.sum(cot[g] * contracted, axis=1))
    for g in each:
        normed, inverse = norm_one[g]
        upstream = input_one_sum[g].reshape(group_shape)
        scale_one_grad.append(jnp.sum(upstream * normed, axis=1))
        shift_one_grad.append(jnp.sum(upstream, axis=1))
        latents_grad.append(
            after_grad[g] + norm_back(normed, inverse, upstream * (1.0 + mods[g][1]))
        )
    block_out = jnp.concatenate(block_out, axis=0)
    latents_grad = jnp.concatenate(latents_grad, axis=0)

    mod_grad = jnp.stack(
        [
            jnp.concatenate(piece, axis=0)
            for piece in (
                shift_one_grad,
                scale_one_grad,
                gate_one_grad,
                shift_two_grad,
                scale_two_grad,
                gate_two_grad,
            )
        ],
        axis=1,
    ).astype(jnp.bfloat16)
    mod_grad_half = lax.dynamic_slice_in_dim(mod_grad, half_here * half_width, half_width, 2)
    all_mod_grad = lax.all_gather(
        mod_grad_half.reshape(latent_count, 6 * half_width), "dp", axis=0, tiled=True
    )
    modulate_grad = tall_dot(cond_low, all_mod_grad).reshape(own_rows, 6, half_width)
    cond_sum = pair_sum(lanes_dot(all_mod_grad, mod_rows).astype(jnp.bfloat16))
    cond_own = local_grad(jax.nn.silu, condition, cond_sum)
    cond_grad = lax.all_to_all(cond_own, "dp", split_axis=0, concat_axis=1, tiled=True)

    def token_sum(pieces):
        return sum(jnp.sum(piece, axis=0, dtype=jnp.float32) for piece in pieces)

    qkv_bias_grad = token_sum(qkv_grad)
    bias_local = jnp.concatenate(
        [
            qkv_bias_grad[:half_width],
            qkv_bias_grad[2 * half_width :],
            token_sum(expand_in),
            token_sum(attn_in),
            token_sum(contract_in),
        ]
    )
    bias_sum = jnp.sum(lax.all_gather(bias_local[None], "dp", axis=0, tiled=True), axis=0)
    split_at = (2 + blocks) * half_width
    units_grad = jnp.concatenate(
        [
            jnp.sum(all_mod_grad, axis=0, dtype=jnp.float32).reshape(6, half_width),
            bias_sum[:split_at].reshape(2 + blocks, half_width),
        ],
        axis=0,
    )
    widths_grad = bias_sum[split_at:].reshape(2, features)
    attend_grad = attend_own.reshape(own_rows, 3, half_width)
    project_grad = project_own.T
    expand_grad = expand_own.reshape(own_rows, blocks, half_width)
    contract_grad = contract_own.reshape(own_rows, blocks, half_width).transpose(1, 2, 0)

    m_mod, s_mod, n_mod = adam(
        modulate_w, modulate_mean, modulate_square, modulate_grad, D ** (-0.5)
    )
    m_att, s_att, n_att = adam(attend_w, attend_mean, attend_square, attend_grad, D ** (-0.5))
    m_proj, s_proj, n_proj = adam(
        output_projection_weight, project_mean, project_square, project_grad, (D // 16) ** (-0.5)
    )
    m_exp, s_exp, n_exp = adam(expand_w, expand_mean, expand_square, expand_grad, D ** (-0.5))
    m_con, s_con, n_con = adam(
        contract_w, contract_mean, contract_square, contract_grad, FF ** (-0.5)
    )
    m_units, s_units, n_units = adam(units_bias, units_mean, units_square, units_grad, 0.15)
    m_widths, s_widths, n_widths = adam(
        output_width_bias, widths_mean, widths_square, widths_grad, 0.15
    )
    return (
        block_out,
        latents_grad,
        cond_grad,
        modulate_grad,
        m_mod,
        s_mod,
        n_mod,
        attend_grad,
        m_att,
        s_att,
        n_att,
        project_grad,
        m_proj,
        s_proj,
        n_proj,
        expand_grad,
        m_exp,
        s_exp,
        n_exp,
        contract_grad,
        m_con,
        s_con,
        n_con,
        units_grad,
        m_units,
        s_units,
        n_units,
        widths_grad,
        m_widths,
        s_widths,
        n_widths,
    )


def solution(mesh):
    placed = (
        P("dp", None, None),
        P("dp", None, None),
        P("dp"),
        P("dp"),
        P(),
        P("dp", None, "tensor"),
        P("dp", None, "tensor"),
        P("tensor", "dp"),
        P("dp", None, "tensor"),
        P(None, "tensor", "dp"),
        P(None, "tensor"),
        P(),
        P("dp", None, "tensor"),
        P("dp", None, "tensor"),
        P("dp", None, "tensor"),
        P("dp", None, "tensor"),
        P("tensor", "dp"),
        P("tensor", "dp"),
        P("dp", None, "tensor"),
        P("dp", None, "tensor"),
        P(None, "tensor", "dp"),
        P(None, "tensor", "dp"),
        P(None, "tensor"),
        P(None, "tensor"),
        P(),
        P(),
    )
    return jax.shard_map(
        on_device,
        mesh=mesh,
        in_specs=placed,
        out_specs=(
            P("dp", None, None),
            P("dp", None, None),
            P("dp", None),
            P("dp", None, "tensor"),
            P("dp", None, "tensor"),
            P("dp", None, "tensor"),
            P("dp", None, "tensor"),
            P("dp", None, "tensor"),
            P("dp", None, "tensor"),
            P("dp", None, "tensor"),
            P("dp", None, "tensor"),
            P("tensor", "dp"),
            P("tensor", "dp"),
            P("tensor", "dp"),
            P("tensor", "dp"),
            P("dp", None, "tensor"),
            P("dp", None, "tensor"),
            P("dp", None, "tensor"),
            P("dp", None, "tensor"),
            P(None, "tensor", "dp"),
            P(None, "tensor", "dp"),
            P(None, "tensor", "dp"),
            P(None, "tensor", "dp"),
            P(None, "tensor"),
            P(None, "tensor"),
            P(None, "tensor"),
            P(None, "tensor"),
            P(),
            P(),
            P(),
            P(),
        ),
        check_vma=False,
    )
```

time: 1640 us -> 966 us (0.59)
  waiting for transfers between devices: 874 us -> 394 us
  local copies, waits for them, and re-layouts: 160 us -> 51.8 us
  Pallas kernels: 0 us -> 73.5 us
  matrix products: 271 us -> 202 us
  blocking collectives: 123 us -> 54.9 us
  other arithmetic: 193 us -> 151 us
  starting transfers between devices: 0.54 us -> 17.4 us
    reduce_scatter x4 -> x3, waiting for transfers between devices: 465 us -> 19.5 us  [scattered(): lax.psum_scatter(local, 'dp', scatter_dimension=0, tiled=True)]
    psum x3 -> x0, waiting for transfers between devices: 285 us -> none  [the longest x1 103 us: on_device(): lax.psum(mlp_part.astype(jnp.bfloat16), 'tensor').astype(jnp.float32)]
    ppermute x0 -> x10, waiting for transfers between devices: none -> 245 us  [swap(): return lax.ppermute(piece, 'tensor', [(0, 1), (1, 0)])]
    pallas_call x0 -> x4, Pallas kernels: none -> 73.5 us  [per_latent(): pl.pallas_call(kernel, grid=(count,), out_shape=jax.ShapeDtypeStruct((cou...]
    dot_general x22 -> x28, matrix products: 271 us -> 202 us  [the longest x9 70 us: rows_dot(): lax.dot_general(left, right, (((1,), (0,)), ((), ())), preferred_element_...]
    psum x2 -> x0, blocking collectives: 68.5 us -> none  [the longest x1 60.1 us: on_device(): units_grad, widths_grad = lax.psum((units_local, widths_local), 'dp')]
    unnamed x14 -> x11, waiting for transfers between devices: 24 us -> 80.1 us
    all_gather x5 -> x4, waiting for transfers between devices: 99.6 us -> 50.2 us  [the longest x1 35.8 us: on_device(): full_attend = lax.all_gather(attend_rows, 'dp', axis=0, tiled=True)]
  transfers between devices with their start and end apart: 13 -> 20, of which waited for: 10 -> 12; matrix products, arithmetic and copies ran while one was open for 24% -> 31% of each run, Pallas kernels for 0% -> 8%
where the time goes in v1:
time: 966 us; the launch traced here: 962 us
  waiting for transfers between devices  394 us (41%)
  matrix products  202 us (21%)
  other arithmetic  151 us (16%)
  Pallas kernels  73.5 us (8%)
  blocking collectives  54.9 us (6%)
  local copies, waits for them, and re-layouts  51.8 us (5%)
  starting transfers between devices  17.4 us (2%)
  between operations  17.3 us (2%)
    ppermute x10, waiting for transfers between devices, swap(): return lax.ppermute(piece, 'tensor', [(0, 1), (1, 0)])  245 us
    unnamed x11, waiting for transfers between devices  80.1 us
    pallas_call x4, Pallas kernels, per_latent(): pl.pallas_call(kernel, grid=(count,), out_shape=jax.ShapeDtypeStruct((cou...  73.5 us
    dot_general x9, matrix products, rows_dot(): lax.dot_general(left, right, (((1,), (0,)), ((), ())), preferred_element_...  70 us
    dot_general x9, matrix products, tall_dot(): lax.dot_general(left, right, (((0,), (0,)), ((), ())), preferred_element_...  65.3 us
    dot_general x9, matrix products, lanes_dot(): lax.dot_general(left, right, (((1,), (1,)), ((), ())), preferred_element_...  64.1 us
    all_gather x1, waiting for transfers between devices, on_device(): full_attend = lax.all_gather(attend_rows, 'dp', axis=0, tiled=True)  35.8 us
    reduce_sum x5, other arithmetic, token_sum(): return sum((jnp.sum(piece, axis=0, dtype=jnp.float32) for piece in pieces))  30.2 us
  transfers between devices with their start and end apart: 20, of which 12 were waited for; matrix products, arithmetic and copies ran while one was open for 31% of the time, Pallas kernels for 8%

profile of v1, /device:TPU:0, one launch (start us, length us, event | category | flops | bytes accessed | tf_op | source)
XLA Modules:
  0.0 961.6 jit_solution(7194047566361967958)
XLA Ops:
  11.0 13.7 %all-reduce.4 = (s32[128]{0:T(128)S(1)}, s32[128]{0:T(128)S(1)}) all-reduce(s32[128]{0:T(128)S(1)} %dynamic-update-slice, s32[128]{0:T(128)S(1)} %dynamic-update-slice.1), channel_id=1, replica_groups=mesh['dp'=16,'tensor'=2] {'dp'}, use_global_device_ids=true, to_apply=%add | all-reduce | flops 256 | bytes 2048
  45.5 79.9 %all-reduce.7.cloned.1.call-done = f32[128,3456]{1,0:T(8,128)} async-done(((f32[128,3456]{1,0:T(8,128)}), f32[128,3456]{1,0:T(8,128)}) %all-reduce.7.cloned.1.call-update) | async-done | bytes 1769488
  142.2 35.8 %all-gather.7.cloned.1.call-done = bf16[1152,1728]{1,0:T(8,128)(2,1)} async-done(((bf16[72,1728]{1,0:T(8,128)(2,1)}), bf16[1152,1728]{1,0:T(8,128)(2,1)}) %all-gather.7.cloned.1.call-update) | async-done | bytes 3981328 | tf_op jit(solution)/shard_map/all_gather | solution.py:226
  191.5 12.8 %shard_map.490 = bf16[4,256,576]{2,1,0:T(8,128)(2,1)S(1)} custom-call(bf16[4,256,1728]{2,1,0:T(8,128)(2,1)S(1)} %bitcast.196), custom_call_target="tpu_custom_call" | custom-call | flops 603979776 | bytes 4718592 | tf_op jit(solution)/shard_map/pallas_call | solution.py:138
  204.3 14.5 %all-gather.9.cloned.1.call-done = bf16[1152,576]{1,0:T(8,128)(2,1)} async-done(((bf16[72,576]{1,0:T(8,128)(2,1)}), bf16[1152,576]{1,0:T(8,128)(2,1)}) %all-gather.9.cloned.1.call-update) | async-done | bytes 1327120 | tf_op jit(solution)/shard_map/all_gather | solution.py:227
  236.2 12.6 %shard_map.489 = bf16[4,256,576]{2,1,0:T(8,128)(2,1)S(1)} custom-call(bf16[4,256,1728]{2,1,0:T(8,128)(2,1)S(1)} %bitcast.198), custom_call_target="tpu_custom_call" | custom-call | flops 603979776 | bytes 4718592 | tf_op jit(solution)/shard_map/pallas_call | solution.py:138
  257.1 21.2 %collective-permute-done.3 = bf16[1024,1152]{1,0:T(8,128)(2,1)} collective-permute-done((bf16[1024,1152]{1,0:T(8,128)(2,1)}, bf16[1024,1152]{1,0:T(8,128)(2,1)}, u32[]{:S(2)}, u32[]{:S(2)}) %collective-permute-start.3) | collective-permute-done | bytes 2359328 | tf_op jit(solution)/shard_map/ppermute | solution.py:70
  278.3 49.9 %collective-permute-done.1 = bf16[1024,1152]{1,0:T(8,128)(2,1)} collective-permute-done((bf16[1024,1152]{1,0:T(8,128)(2,1)S(1)}, bf16[1024,1152]{1,0:T(8,128)(2,1)}, u32[]{:S(2)}, u32[]{:S(2)}) %collective-permute-start.1) | collective-permute-done | bytes 2359328 | tf_op jit(solution)/shard_map/ppermute | solution.py:70
  361.9 15.0 %convert_reduce_fusion.1 = (f32[2304]{0:T(1024)}, bf16[1024,2304]{1,0:T(8,128)(2,1)S(1)}) fusion(f32[1024,2304]{1,0:T(8,128)} %fusion.70, f32[2304]{0:T(1024)S(1)} %add.408, bf16[1024,1152]{1,0:T(8,128)(2,1)S(1)} %bitcast.234, bf16[1152,2304]{1,0:T(8,128)(2,1)} %all-gather.13.cloned.1.call-done), kind=kOutput, calls=%fused_computation.25 | convolution fusion | flops 5490079744 | bytes 21841920 | tf_op jit(solution)/shard_map/dot_general | solution.py:78
  419.5 18.1 %collective-permute-done.5 = bf16[1024,1152]{1,0:T(8,128)(2,1)S(1)} collective-permute-done((bf16[1024,1152]{1,0:T(8,128)(2,1)S(1)}, bf16[1024,1152]{1,0:T(8,128)(2,1)S(1)}, u32[]{:S(2)}, u32[]{:S(2)}) %collective-permute-start.5) | collective-permute-done | bytes 2359328 | tf_op jit(solution)/shard_map/ppermute | solution.py:70
  446.9 41.5 %collective-permute-done.2 = bf16[1024,1152]{1,0:T(8,128)(2,1)} collective-permute-done((bf16[1024,1152]{1,0:T(8,128)(2,1)}, bf16[1024,1152]{1,0:T(8,128)(2,1)}, u32[]{:S(2)}, u32[]{:S(2)}) %collective-permute-start.2) | collective-permute-done | bytes 2359328 | tf_op jit(solution)/shard_map/ppermute | solution.py:70
  488.3 48.9 %collective-permute-done.4 = bf16[1024,1152]{1,0:T(8,128)(2,1)} collective-permute-done((bf16[1024,1152]{1,0:T(8,128)(2,1)}, bf16[1024,1152]{1,0:T(8,128)(2,1)}, u32[]{:S(2)}, u32[]{:S(2)}) %collective-permute-start.4) | collective-permute-done | bytes 2359328 | tf_op jit(solution)/shard_map/ppermute | solution.py:70
  537.3 14.0 %convert_reduce_fusion.7 = (f32[1152]{0:T(1024)}, bf16[4,256,1152]{2,1,0:T(8,128)(2,1)}, f32[4,256,1152]{2,1,0:T(8,128)}, bf16[4,1152]{1,0:T(4,128)(2,1)}, f32[1...) fusion(f32[4,1152]{1,0:T(4,128)S(1)} %bitcast.247, ...), kind=kLoop, calls=%fused_computation.59 | loop fusion | flops 36557568 | bytes 47289856 | tf_op jit(solution)/shard_map/reduce_sum | solution.py:364
  551.3 15.5 %convert_reduce_fusion = (f32[2304]{0:T(1024)}, bf16[1024,2304]{1,0:T(8,128)(2,1)S(1)}) fusion(f32[1024,2304]{1,0:T(8,128)} %fusion.71, f32[2304]{0:T(1024)S(1)} %add.408, bf16[1024,1152]{1,0:T(8,128)(2,1)} %bitcast.232, bf16[1152,2304]{1,0:T(8,128)(2,1)} %all-gather.13.cloned.1.call-done), kind=kOutput, calls=%fused_computation.24 | convolution fusion | flops 5490079744 | bytes 21841920 | tf_op jit(solution)/shard_map/dot_general | solution.py:78
  592.4 37.3 %collective-permute-done.7 = bf16[1024,1152]{1,0:T(8,128)(2,1)S(1)} collective-permute-done((bf16[1024,1152]{1,0:T(8,128)(2,1)S(1)}, bf16[1024,1152]{1,0:T(8,128)(2,1)S(1)}, u32[]{:S(2)}, u32[]{:S(2)}) %collective-permute-start.7) | collective-permute-done | bytes 2359328 | tf_op jit(solution)/shard_map/ppermute | solution.py:70
  648.9 12.3 %fusion.1 = bf16[1152,2304]{1,0:T(8,128)(2,1)} fusion(f32[1152,2304]{1,0:T(8,128)} %fusion.54, bf16[1024,1152]{1,0:T(8,128)(2,1)S(1)} %bitcast.233, f32[1024,2304]{1,0:T(8,128)} %fusion.71, f32[2304]{0:T(1024)S(1)} %add.408), kind=kOutput, calls=%fused_computation.7 | convolution fusion | flops 5464719360 | bytes 27730944 | tf_op jit(solution)/shard_map/dot_general | solution.py:90
  687.0 24.1 %shard_map.491 = bf16[4,256,1728]{2,1,0:T(8,128)(2,1)S(1)} custom-call(bf16[4,256,1728]{2,1,0:T(8,128)(2,1)} %bitcast.197, bf16[4,256,576]{2,1,0:T(8,128)(2,1)S(1)} %bitcast.201), custom_call_target="tpu_custom_call" | custom-call | flops 1811939328 | bytes 8257536 | tf_op jit(solution)/shard_map/pallas_call | solution.py:138
  734.9 23.9 %shard_map.492 = bf16[4,256,1728]{2,1,0:T(8,128)(2,1)S(1)} custom-call(bf16[4,256,1728]{2,1,0:T(8,128)(2,1)} %bitcast.195, bf16[4,256,576]{2,1,0:T(8,128)(2,1)S(1)} %bitcast.202), custom_call_target="tpu_custom_call" | custom-call | flops 1811939328 | bytes 8257536 | tf_op jit(solution)/shard_map/pallas_call | solution.py:138
  761.4 21.1 %all-gather.1 = f32[16,1,5760]{2,1,0:T(1,128)S(1)} all-gather(f32[1,1,5760]{2,1,0:T(1,128)S(1)} %reshape.376), channel_id=2, replica_groups=mesh['dp'=16,'tensor'=2] {'dp'}, dimensions={0}, use_global_device_ids=true | all-gather | bytes 391680 | tf_op jit(solution)/shard_map/all_gather | solution.py:376
  797.2 12.2 %fusion.17 = bf16[1152,1728]{1,0:T(8,128)(2,1)} fusion(f32[1152,1728]{1,0:T(8,128)} %convolution_bitcast_fusion.1, bf16[4,256,1152]{2,1,0:T(8,128)(2,1)} %get-tuple-element.268, bf16[4,256,1728]{2,1,0:T(8,128)(2,1)} %copy-done.2), kind=kOutput, calls=%fused_computation.31 | convolution fusion | flops 4080844800 | bytes 17842176 | tf_op jit(solution)/shard_map/dot_general | solution.py:90
  821.0 23.8 %collective-permute-done.8 = bf16[1024,1152]{1,0:T(8,128)(2,1)} collective-permute-done((bf16[1024,1152]{1,0:T(8,128)(2,1)S(1)}, bf16[1024,1152]{1,0:T(8,128)(2,1)}, u32[]{:S(2)}, u32[]{:S(2)}) %collective-permute-start.8) | collective-permute-done | bytes 2359328 | tf_op jit(solution)/shard_map/ppermute | solution.py:70
  855.7 14.5 %multiply_add_fusion.2 = (f32[4,256,1152]{2,1,0:T(8,128)}, f32[4,256,1152]{2,1,0:T(8,128)}, bf16[4,1152]{1,0:T(4,128)(2,1)S(1)}) fusion(f32[4,256,1152]{2,1,0:T(8,128)} %get-tuple-element.228, f32[4,256]{1,0:T(4,128)S(1)} %broadcast_multiply_fusion.6, f32[4,256]{1,0:T(4,128)S(1)} %div.152, f32[4,1152]{1,0:T(4,128)S(1)} %copy-done.47, ...), kind=kLoop, calls=%fused_computation.72 | loop fusion | flops 28306944 | bytes 42546176 | tf_op jit(solution)/shard_map/add | solution.py:335
  870.7 20.1 %all_gather.30 = bf16[128,3456]{1,0:T(8,128)(2,1)S(1)} all-gather(bf16[8,3456]{1,0:T(8,128)(2,1)S(1)} %reshape.355), channel_id=1, replica_groups=mesh['dp'=16,'tensor'=2] {'dp'}, dimensions={0}, use_global_device_ids=true | all-gather | bytes 940032 | tf_op jit(solution)/shard_map/all_gather | solution.py:355
  931.4 19.5 %reduce-scatter.7.cloned.1.call-done = bf16[72,1728]{1,0:T(8,128)(2,1)} async-done(((bf16[1152,1728]{1,0:T(8,128)(2,1)}), bf16[72,1728]{1,0:T(8,128)(2,1)}) %reduce-scatter.7.cloned.1.call-update) | async-done | bytes 248848 | tf_op jit(solution)/shard_map/reduce_scatter | solution.py:292
  (454 shorter events, 342.0 us)
Async XLA Ops:
  7.2 118.2 %all-reduce.7.cloned.1.call-start = ((), (), s32[]{:S(2)}) async-start(), calls=%async_computation.12 | async-start | bytes 3538944
  31.2 146.8 %all-gather.7.cloned.1.call-start = ((), (), s32[]{:S(2)}) async-start(), calls=%async_computation.5 | async-start | bytes 4386816 | tf_op jit(solution)/shard_map/all_gather | solution.py:226
  32.4 186.4 %all-gather.9.cloned.1.call-start = ((), (), s32[]{:S(2)}) async-start(), calls=%async_computation.6 | async-start | bytes 1566720 | tf_op jit(solution)/shard_map/all_gather | solution.py:227
  33.1 317.1 %all-gather.11.cloned.1.call-start = ((), (), s32[]{:S(2)}) async-start(), calls=%async_computation.7 | async-start | bytes 5640192 | tf_op jit(solution)/shard_map/all_gather | solution.py:228
  34.4 327.5 %all-gather.13.cloned.1.call-start = ((), (), s32[]{:S(2)}) async-start(), calls=%async_computation.8 | async-start | bytes 5640192 | tf_op jit(solution)/shard_map/all_gather | solution.py:229
  35.7 783.3 %reduce-scatter.13.cloned.1.call-start = ((), (), s32[]{:S(2)}) async-start(), calls=%async_computation.13 | async-start | bytes 1566720
  44.8 97.4 %copy-start.74 = (f32[4,256]{1,0:T(4,128)}, f32[4,256]{1,0:T(4,128)S(1)}, u32[]{:S(2)}) copy-start(f32[4,256]{1,0:T(4,128)S(1)} %add_rsqrt_fusion.1) | copy-start | bytes 12292
  44.9 97.4 %copy-start.76 = (f32[4,256]{1,0:T(4,128)}, f32[4,256]{1,0:T(4,128)S(1)}, u32[]{:S(2)}) copy-start(f32[4,256]{1,0:T(4,128)S(1)} %add_rsqrt_fusion.3) | copy-start | bytes 12292
  126.5 5.4 collective-permute-start
  223.9 54.4 %collective-permute-start.3 = (bf16[1024,1152]{1,0:T(8,128)(2,1)}, bf16[1024,1152]{1,0:T(8,128)(2,1)}, u32[]{:S(2)}, u32[]{:S(2)}) collective-permute-start(bf16[1024,1152]{1,0:T(8,128)(2,1)} %convolution_convert_fusion.6), channel_id=1, source_target_pairs={{0,1},{1,0},{2,3},{3,2},{4,5},{5,4},{6,7},{7,6},{8,9},{9,8},{10,11... | collective-permute-start | bytes 7077896 | tf_op jit(solution)/shard_map/ppermute | solution.py:70
  251.2 77.0 %collective-permute-start.1 = (bf16[1024,1152]{1,0:T(8,128)(2,1)S(1)}, bf16[1024,1152]{1,0:T(8,128)(2,1)}, u32[]{:S(2)}, u32[]{:S(2)}) collective-permute-start(bf16[1024,1152]{1,0:T(8,128)(2,1)S(1)} %convolution_convert_fusion.7), channel_id=1, source_target_pairs={{0,1},{1,0},{2,3},{3,2},{4,5},{5,4},{6,7},{7,6},{8,9},{9,8},{10,11... | collective-permute-start | bytes 7077896 | tf_op jit(solution)/shard_map/ppermute | solution.py:70
  383.4 54.3 %collective-permute-start.5 = (bf16[1024,1152]{1,0:T(8,128)(2,1)S(1)}, bf16[1024,1152]{1,0:T(8,128)(2,1)S(1)}, u32[]{:S(2)}, u32[]{:S(2)}) collective-permute-start(bf16[1024,1152]{1,0:T(8,128)(2,1)S(1)} %convolution_convert_fusion.1), channel_id=1, source_target_pairs={{0,1},{1,0},{2,3},{3,2},{4,5},{5,4},{6,7},{7,6},{8,9},{9,8},{10,11... | collective-permute-start | bytes 7077896 | tf_op jit(solution)/shard_map/ppermute | solution.py:70
  397.0 91.3 %collective-permute-start.2 = (bf16[1024,1152]{1,0:T(8,128)(2,1)}, bf16[1024,1152]{1,0:T(8,128)(2,1)}, u32[]{:S(2)}, u32[]{:S(2)}) collective-permute-start(bf16[1024,1152]{1,0:T(8,128)(2,1)} %convolution_convert_fusion.3), channel_id=1, source_target_pairs={{0,1},{1,0},{2,3},{3,2},{4,5},{5,4},{6,7},{7,6},{8,9},{9,8},{10,11... | collective-permute-start | bytes 7077896 | tf_op jit(solution)/shard_map/ppermute | solution.py:70
  418.1 119.2 %collective-permute-start.4 = (bf16[1024,1152]{1,0:T(8,128)(2,1)}, bf16[1024,1152]{1,0:T(8,128)(2,1)}, u32[]{:S(2)}, u32[]{:S(2)}) collective-permute-start(bf16[1024,1152]{1,0:T(8,128)(2,1)} %convolution_convert_fusion.2), channel_id=1, source_target_pairs={{0,1},{1,0},{2,3},{3,2},{4,5},{5,4},{6,7},{7,6},{8,9},{9,8},{10,11... | collective-permute-start | bytes 7077896 | tf_op jit(solution)/shard_map/ppermute | solution.py:70
  437.7 99.6 %slice-start.3 = ((s8[4718592]{0:T(1024)(128)(4,1)}), s8[524288]{0:T(1024)(128)(4,1)S(1)}, s32[]{:S(2)}) async-start(s8[4718592]{0:T(1024)(128)(4,1)} %bitcast.207), calls=%async_computation.17 | async-start | bytes 1048576
  440.6 96.6 %slice-start.4 = ((s8[4718592]{0:T(1024)(128)(4,1)}), s8[4194304]{0:T(1024)(128)(4,1)S(1)}, s32[]{:S(2)}) async-start(s8[4718592]{0:T(1024)(128)(4,1)} %bitcast.207), calls=%async_computation.18 | async-start | bytes 8388608
  578.1 51.7 %collective-permute-start.7 = (bf16[1024,1152]{1,0:T(8,128)(2,1)S(1)}, bf16[1024,1152]{1,0:T(8,128)(2,1)S(1)}, u32[]{:S(2)}, u32[]{:S(2)}) collective-permute-start(bf16[1024,1152]{1,0:T(8,128)(2,1)S(1)} %convolution_convert_fusion), channel_id=1, source_target_pairs={{0,1},{1,0},{2,3},{3,2},{4,5},{5,4},{6,7},{7,6},{8,9},{9,8},{10,11... | collective-permute-start | bytes 7077896 | tf_op jit(solution)/shard_map/ppermute | solution.py:70
  648.9 273.5 %reduce-scatter.11.cloned.1.call-start = ((), (), s32[]{:S(2)}) async-start(), calls=%async_computation.11 | async-start | bytes 5640192 | tf_op jit(solution)/shard_map/reduce_scatter | solution.py:292
  661.3 262.7 %reduce-scatter.9.cloned.1.call-start = ((), (), s32[]{:S(2)}) async-start(), calls=%async_computation.10 | async-start | bytes 5640192 | tf_op jit(solution)/shard_map/reduce_scatter | solution.py:292
  681.1 269.9 %reduce-scatter.7.cloned.1.call-start = ((), (), s32[]{:S(2)}) async-start(), calls=%async_computation.9 | async-start | bytes 4386816 | tf_op jit(solution)/shard_map/reduce_scatter | solution.py:292
  719.6 72.1 %collective-permute-start.6 = (bf16[1024,1152]{1,0:T(8,128)(2,1)}, bf16[1024,1152]{1,0:T(8,128)(2,1)}, u32[]{:S(2)}, u32[]{:S(2)}) collective-permute-start(bf16[1024,1152]{1,0:T(8,128)(2,1)} %convolution_convert_fusion.5), channel_id=1, source_target_pairs={{0,1},{1,0},{2,3},{3,2},{4,5},{5,4},{6,7},{7,6},{8,9},{9,8},{10,11... | collective-permute-start | bytes 7077896 | tf_op jit(solution)/shard_map/ppermute | solution.py:70
  791.1 53.7 %collective-permute-start.8 = (bf16[1024,1152]{1,0:T(8,128)(2,1)S(1)}, bf16[1024,1152]{1,0:T(8,128)(2,1)}, u32[]{:S(2)}, u32[]{:S(2)}) collective-permute-start(bf16[1024,1152]{1,0:T(8,128)(2,1)S(1)} %convolution_convert_fusion.4), channel_id=1, source_target_pairs={{0,1},{1,0},{2,3},{3,2},{4,5},{5,4},{6,7},{7,6},{8,9},{9,8},{10,11... | collective-permute-start | bytes 7077896 | tf_op jit(solution)/shard_map/ppermute | solution.py:70
  893.2 14.1 %collective-permute-start.9 = (bf16[128,72]{0,1:T(8,128)(2,1)S(1)}, bf16[128,72]{0,1:T(8,128)(2,1)S(1)}, u32[]{:S(2)}, u32[]{:S(2)}) collective-permute-start(bf16[128,72]{0,1:T(8,128)(2,1)S(1)} %convolution_convert_fusion.10), channel_id=1, source_target_pairs={{0,1},{1,0},{2,3},{3,2},{4,5},{5,4},{6,7},{7,6},{8,9},{9,8},{10,11... | collective-permute-start | bytes 55304 | tf_op jit(solution)/shard_map/ppermute | solution.py:70
  908.1 12.7 %all-to-all-start = ((f32[16,8,72]{2,1,0:T(8,128)}), f32[16,8,72]{2,1,0:T(8,128)}, u32[]{:S(2)}, u32[]{:S(2)}) async-start(f32[16,8,72]{2,1,0:T(8,128)} %bitcast.37), calls=%async_computation | async-start | bytes 131072 | tf_op jit(solution)/shard_map/all_to_all | solution.py:361
  (124 other events, 2102.0 us)
Sparse Core Ops, SparseCore 0:
  31.3 94.1 all-reduce.6
  128.6 49.3 all-gather.6
  180.9 37.8 all-gather.8
  221.6 55.1 all-gather.10
  279.7 54.9 all-gather.12
  649.0 57.4 reduce-scatter.12
  711.1 79.5 reduce-scatter.10
  795.3 79.4 reduce-scatter.8
  879.3 71.6 reduce-scatter.6
